TPU v7x, 256 devices: a whole 4x4x8 slice. The times are simulated.
256 devices in a mesh: chan: 32 (over x_hi, z, core), freq: 8 (over x_lo, y).
Axes of the slice: x: 4 (x_hi: 2, x_lo: 2; x = x_hi * 2 + x_lo), y: 4, z: 8, core: 2. Of those that a mesh axis runs over, the one named last changes fastest.
Arguments:
- spectra: bfloat16 [2, 2, 2048, 16384], P(None, None, 'freq', 'chan'), may hold values from -6 to 6
- gap: int32 [16384], P('chan'), may hold values 0 or 1
- reach: int32 [128], P('chan'), may hold values from 1 to 8, as said below
- valid: int32 [128, 8], P('chan'), may hold values 0 or 1
Outputs:
- upper: float32 [128, 128, 8, 2, 128], P('freq', 'chan')
- lower: float32 [128, 128, 8, 2, 128], P('freq', 'chan')
Inputs may be any that keep to these rules, and one draw needn't show every extreme that they name: reach of some block equals 8 in every draw.
All inputs are finite; a program needn't handle non-finite values. No bound on the sum of `gap` or of `valid` on one device may be relied on, other than what follows from the above.
Results may differ from a plain program's by a relative error of at most 0.0003.
Values may be sent and summed in bfloat16 or wider, within the bound.
A program may use at most 64 MiB of HBM per device.

v0:
```python
import math

import jax
import jax.numpy as jnp
from jax import lax
from jax.sharding import PartitionSpec as P

BINS = 2048
SEGS = 2
KOFF = 8


def shifted(value, axis, steps):
    count = lax.axis_size(axis)
    initial, last = (max(0, -steps), min(count, count - steps))
    return lax.ppermute(value, axis, [(source, source + steps) for source in range(initial, last)])


def turned_rows(window, depth, count, width):
    twin = jnp.concatenate([window[1:2], -window[0:1]], axis=0)
    return twin.reshape(depth, count, width)


def shards(spectra, gap, reach, valid):
    blocks_here = reach.shape[0]
    width = spectra.shape[3] // blocks_here
    depth = spectra.shape[0] * spectra.shape[1] * spectra.shape[2]
    lanes = lax.axis_size("chan")
    place = lax.axis_index("chan")
    scale = 1.0 / math.sqrt(SEGS * BINS)
    hops = (KOFF + blocks_here - 2) // blocks_here
    masked = spectra * gap.astype(jnp.bfloat16)
    offsets = jnp.arange(KOFF)
    global_first = place * blocks_here + jnp.arange(blocks_here)
    weight = (offsets[None, :] < reach[:, None]) & (valid > 0)
    weight = weight & (global_first[:, None] + offsets[None, :] < lanes * blocks_here)
    weight = weight.astype(jnp.float32)
    own = masked.reshape(depth, blocks_here, width)
    ahead = [shifted(masked, "chan", -(step + 1)) for step in range(hops)]
    window = jnp.concatenate([masked] + ahead, axis=3)
    span = (hops + 1) * blocks_here
    wide = window.reshape(depth, span, width)
    wide_twin = turned_rows(window, depth, span, width)
    per_offset = []
    for upper_k in range(KOFF):
        real = jnp.einsum(
            "cbi,cbj->ibj",
            own,
            wide[:, upper_k : upper_k + blocks_here],
            preferred_element_type=jnp.float32,
        )
        imag = jnp.einsum(
            "cbi,cbj->ibj",
            own,
            wide_twin[:, upper_k : upper_k + blocks_here],
            preferred_element_type=jnp.float32,
        )
        per_offset.append(jnp.stack([real, imag], axis=2) * scale)
    terms = jnp.stack(per_offset, axis=2)
    upper = lax.psum_scatter(
        terms * weight[None, :, :, None, None], "freq", scatter_dimension=0, tiled=True
    )
    behind = [shifted(upper, "chan", step + 1) for step in range(hops)]
    sources = [upper] + behind
    sign = jnp.array([1.0, -1.0], dtype=jnp.float32)
    columns = []
    for target in range(blocks_here):
        picked = []
        for k in range(KOFF):
            gap_index = target - k
            source = sources[-(gap_index // blocks_here)]
            picked.append(source[:, gap_index % blocks_here, k])
        columns.append(jnp.stack(picked, axis=1))
    lower = jnp.stack(columns, axis=1) * sign[None, None, None, :, None]
    return (upper, lower)


def solution(mesh):
    placed = (P(None, None, "freq", "chan"), P("chan"), P("chan"), P("chan", None))
    return jax.shard_map(
        shards,
        mesh=mesh,
        in_specs=placed,
        out_specs=(P("freq", "chan", None, None, None), P("freq", "chan", None, None, None)),
        check_vma=False,
    )
```

profile of v0, /device:TPU:6, one launch (start us, length us, event | category | flops | bytes accessed | tf_op | source)
XLA Modules:
  0.0 187.7 jit_solution(11123553173537422763)
XLA Ops:
  7.2 0.7 convert_element_type.6
  7.9 1.3 broadcast_multiply_fusion.1
  9.2 8.6 %collective-permute-start.1 = (bf16[2,2,256,512]{3,2,1,0:T(8,128)(2,1)S(1)}, bf16[2,2,256,512]{3,2,1,0:T(8,128)(2,1)S(1)}, u32[]{:S(2)}, u32[]{:S(2)}) collective-permute-start(bf16[2,2,256,512]{3,2,1,0:T(8,128)(2,1)S(1)} %broadcast_multiply_fusion.1), channel_id=1, source_target_pairs={{16,0},{24,8},{32,16},{40,24},{48,32},{56,40},{64,48},{72,56},{80,... | collective-permute-start | bytes 3145736 | tf_op jit(solution)/shard_map/ppermute | solution.py:16
  17.8 2.1 %collective-permute-start = (bf16[2,2,256,512]{3,2,1,0:T(8,128)(2,1)S(1)}, bf16[2,2,256,512]{3,2,1,0:T(8,128)(2,1)}, u32[]{:S(2)}, u32[]{:S(2)}) collective-permute-start(bf16[2,2,256,512]{3,2,1,0:T(8,128)(2,1)S(1)} %broadcast_multiply_fusion.1), channel_id=1, source_target_pairs={{8,0},{16,8},{24,16},{32,24},{40,32},{48,40},{56,48},{64,56},{72,6... | collective-permute-start | bytes 3145736 | tf_op jit(solution)/shard_map/ppermute | solution.py:16
  19.9 1.1 reshape.270
  21.2 19.0 %collective-permute-done.1 = bf16[2,2,256,512]{3,2,1,0:T(8,128)(2,1)S(1)} collective-permute-done((bf16[2,2,256,512]{3,2,1,0:T(8,128)(2,1)S(1)}, bf16[2,2,256,512]{3,2,1,0:T(8,128)(2,1)S(1)}, u32[]{:S(2)}, u32[]{:S(2)}) %collective-permute-start.1) | collective-permute-done | bytes 1048608 | tf_op jit(solution)/shard_map/ppermute | solution.py:16
  40.2 1.0 copy-done.10
  41.2 10.2 %collective-permute-done = bf16[2,2,256,512]{3,2,1,0:T(8,128)(2,1)} collective-permute-done((bf16[2,2,256,512]{3,2,1,0:T(8,128)(2,1)S(1)}, bf16[2,2,256,512]{3,2,1,0:T(8,128)(2,1)}, u32[]{:S(2)}, u32[]{:S(2)}) %collective-permute-start) | collective-permute-done | bytes 1048608 | tf_op jit(solution)/shard_map/ppermute | solution.py:16
  51.5 2.0 %pad_maximum_fusion = bf16[2,2,256,1536]{3,2,1,0:T(8,128)(2,1)S(1)} fusion(bf16[2,2,256,512]{3,2,1,0:T(8,128)(2,1)} %copy-done.10, bf16[2,2,256,512]{3,2,1,0:T(8,128)(2,1)} %collective-permute-done, bf16[2,2,256,512]{3,2,1,0:T(8,128)(2,1)} %copy-done.2), kind=kLoop, calls=%fused_computation | loop fusion | flops 9437184 | bytes 6291456 | tf_op jit(solution)/shard_map/concatenate | solution.py:40
  53.4 5.8 %copy.39 = bf16[2,2,256,1536]{2,1,0,3:T(2,128)(2,1)} copy(bf16[2,2,256,1536]{3,2,1,0:T(8,128)(2,1)S(1)} %pad_maximum_fusion) | data formatting | bytes 6291456 | tf_op jit(solution)/shard_map/concatenate | solution.py:40
  59.2 0.2 fusion.27
  59.4 0.3 pad_maximum_fusion.1
  59.7 5.8 %copy.41 = bf16[2,2,256,1536]{2,1,0,3:T(2,128)(2,1)} copy(bf16[2,2,256,1536]{3,2,1,0:T(8,128)(2,1)S(1)} %pad_maximum_fusion.1) | data formatting | bytes 6291456 | tf_op jit(solution)/shard_map/concatenate | solution.py:20
  65.5 4.7 %reshape.271 = bf16[1024,12,128]{0,2,1:T(8,128)(2,1)S(1)} reshape(bf16[2,2,256,1536]{2,1,0,3:T(2,128)(2,1)} %copy.41) | data formatting | bytes 6291456 | tf_op jit(solution)/shard_map/reshape | solution.py:21
  70.2 1.7 convolution_bitcast_fusion
  72.0 1.1 convolution_bitcast_fusion.2
  73.1 1.2 convolution_bitcast_fusion.4
  74.3 1.1 convolution_bitcast_fusion.6
  75.4 1.2 convolution_bitcast_fusion.8
  76.6 1.2 convolution_bitcast_fusion.10
  77.7 1.2 convolution_bitcast_fusion.12
  78.9 1.2 convolution_bitcast_fusion.14
  80.0 4.7 %reshape.269 = bf16[1024,12,128]{0,2,1:T(8,128)(2,1)S(1)} reshape(bf16[2,2,256,1536]{2,1,0,3:T(2,128)(2,1)} %copy.39) | data formatting | bytes 6291456 | tf_op jit(solution)/shard_map/reshape | solution.py:42
  84.7 1.7 convolution_bitcast_fusion.1
  86.5 0.4 convolution_bitcast_fusion.3
  86.9 0.4 convolution_bitcast_fusion.5
  87.4 0.4 convolution_bitcast_fusion.7
  87.9 0.4 convolution_bitcast_fusion.9
  88.3 0.4 convolution_bitcast_fusion.11
  88.8 0.4 convolution_bitcast_fusion.13
  89.3 0.4 convolution_bitcast_fusion.15
  89.7 0.5 copy-done.9
  90.5 0.7 copy-done.5
  91.4 2.4 %broadcast_multiply_fusion = f32[128,4,8,2,128]{0,4,1,3,2:T(8,128)} fusion(f32[128,4,8,2,128]{0,4,1,3,2:T(8,128)S(1)} %fusion.7, f32[4,8]{0,1:T(8,128)S(1)} %copy.57), kind=kLoop, calls=%fused_computation.2 | loop fusion | flops 1048576 | bytes 8388736 | tf_op jit(solution)/shard_map/mul | solution.py:61
  93.8 5.5 %copy.58 = f32[128,4,8,2,128]{4,2,3,1,0:T(8,128)} copy(f32[128,4,8,2,128]{0,4,1,3,2:T(8,128)} %broadcast_multiply_fusion) | data formatting | bytes 8388608 | tf_op jit(solution)/shard_map/mul | solution.py:61
  99.3 54.2 %reduce-scatter.2.cloned.1.call-done = f32[16,4,8,2,128]{4,2,3,1,0:T(8,128)} async-done(((f32[128,4,8,2,128]{4,2,3,1,0:T(8,128)}), f32[16,4,8,2,128]{4,2,3,1,0:T(8,128)}) %reduce-scatter.2.cloned.1.call-update) | async-done | bytes 524304 | tf_op jit(solution)/shard_map/reduce_scatter | solution.py:60
  153.5 3.4 %collective-permute-start.3 = (f32[16,4,8,2,128]{4,2,3,1,0:T(8,128)}, f32[16,4,8,2,128]{4,2,3,1,0:T(8,128)S(1)}, u32[]{:S(2)}, u32[]{:S(2)}) collective-permute-start(f32[16,4,8,2,128]{4,2,3,1,0:T(8,128)} %reduce-scatter.2.cloned.1.call-done), channel_id=1, source_target_pairs={{0,16},{8,24},{16,32},{24,40},{32,48},{40,56},{48,64},{56,72},{64,... | collective-permute-start | bytes 1572872 | tf_op jit(solution)/shard_map/ppermute | solution.py:16
  157.0 1.9 %collective-permute-start.2 = (f32[16,4,8,2,128]{4,2,3,1,0:T(8,128)}, f32[16,4,8,2,128]{4,2,3,1,0:T(8,128)S(1)}, u32[]{:S(2)}, u32[]{:S(2)}) collective-permute-start(f32[16,4,8,2,128]{4,2,3,1,0:T(8,128)} %reduce-scatter.2.cloned.1.call-done), channel_id=1, source_target_pairs={{0,8},{8,16},{16,24},{24,32},{32,40},{40,48},{48,56},{56,64},{64,7... | collective-permute-start | bytes 1572872 | tf_op jit(solution)/shard_map/ppermute | solution.py:16
  158.9 2.1 %copy.95 = f32[16,4,8,2,128]{4,3,2,1,0:T(2,128)} copy(f32[16,4,8,2,128]{4,2,3,1,0:T(8,128)} %reduce-scatter.2.cloned.1.call-done) | data formatting | bytes 1048576
  161.0 1.5 slice_bitcast_fusion.31
  162.6 11.5 %collective-permute-done.3 = f32[16,4,8,2,128]{4,2,3,1,0:T(8,128)S(1)} collective-permute-done((f32[16,4,8,2,128]{4,2,3,1,0:T(8,128)}, f32[16,4,8,2,128]{4,2,3,1,0:T(8,128)S(1)}, u32[]{:S(2)}, u32[]{:S(2)}) %collective-permute-start.3) | collective-permute-done | bytes 524320 | tf_op jit(solution)/shard_map/ppermute | solution.py:16
  174.1 4.4 %collective-permute-done.2 = f32[16,4,8,2,128]{4,2,3,1,0:T(8,128)S(1)} collective-permute-done((f32[16,4,8,2,128]{4,2,3,1,0:T(8,128)}, f32[16,4,8,2,128]{4,2,3,1,0:T(8,128)S(1)}, u32[]{:S(2)}, u32[]{:S(2)}) %collective-permute-start.2) | collective-permute-done | bytes 524320 | tf_op jit(solution)/shard_map/ppermute | solution.py:16
  178.6 0.3 slice_bitcast_fusion.27
  178.8 0.2 stack.135
  179.0 0.2 stack.141
  179.2 0.2 stack.139
  179.4 0.2 stack.137
  179.8 1.1 copy.96
  (40 shorter events, 0.9 us)
Async XLA Ops:
  7.2 13.9 %copy-start.11 = (s32[4,8]{1,0:T(4,128)S(1)}, s32[4,8]{1,0:T(4,128)}, u32[]{:S(2)}) copy-start(s32[4,8]{1,0:T(4,128)} %param.8) | copy-start | bytes 388
  7.2 13.9 %copy-start.13 = (s32[4]{0:T(128)S(1)}, s32[4]{0:T(128)}, u32[]{:S(2)}) copy-start(s32[4]{0:T(128)} %param.7) | copy-start | bytes 52
  7.2 146.3 %reduce-scatter.2.cloned.1.call-start = ((), (), s32[]{:S(2)}) async-start(), calls=%async_computation.1 | async-start | bytes 4718592 | tf_op jit(solution)/shard_map/reduce_scatter | solution.py:60
  9.2 31.0 %copy-start.2 = (bf16[2,2,256,512]{3,2,1,0:T(8,128)(2,1)}, bf16[2,2,256,512]{3,2,1,0:T(8,128)(2,1)S(1)}, u32[]{:S(2)}) copy-start(bf16[2,2,256,512]{3,2,1,0:T(8,128)(2,1)S(1)} %broadcast_multiply_fusion.1) | copy-start | bytes 3145732
  9.2 31.0 %collective-permute-start.1 = (bf16[2,2,256,512]{3,2,1,0:T(8,128)(2,1)S(1)}, bf16[2,2,256,512]{3,2,1,0:T(8,128)(2,1)S(1)}, u32[]{:S(2)}, u32[]{:S(2)}) collective-permute-start(bf16[2,2,256,512]{3,2,1,0:T(8,128)(2,1)S(1)} %broadcast_multiply_fusion.1), channel_id=1, source_target_pairs={{16,0},{24,8},{32,16},{40,24},{48,32},{56,40},{64,48},{72,56},{80,... | collective-permute-start | bytes 3145736 | tf_op jit(solution)/shard_map/ppermute | solution.py:16
  17.8 33.6 %collective-permute-start = (bf16[2,2,256,512]{3,2,1,0:T(8,128)(2,1)S(1)}, bf16[2,2,256,512]{3,2,1,0:T(8,128)(2,1)}, u32[]{:S(2)}, u32[]{:S(2)}) collective-permute-start(bf16[2,2,256,512]{3,2,1,0:T(8,128)(2,1)S(1)} %broadcast_multiply_fusion.1), channel_id=1, source_target_pairs={{8,0},{16,8},{24,16},{32,24},{40,32},{48,40},{56,48},{64,56},{72,6... | collective-permute-start | bytes 3145736 | tf_op jit(solution)/shard_map/ppermute | solution.py:16
  40.2 1.0 copy-start.10
  70.2 1.8 copy-start
  84.7 1.8 copy-start.1
  89.2 1.0 copy-start.9
  89.2 1.0 copy-start.8
  89.2 1.1 copy-start.7
  89.3 1.2 copy-start.6
  90.2 1.0 copy-start.5
  90.2 1.1 copy-start.4
  90.2 1.2 copy-start.3
  99.3 80.3 %copy-start.12 = (f32[2]{0:T(128)S(1)}, f32[2]{0:T(128)}, u32[]{:S(2)}) copy-start(f32[2]{0:T(128)} %constant.16.clone) | copy-start | bytes 28
  153.5 20.5 %collective-permute-start.3 = (f32[16,4,8,2,128]{4,2,3,1,0:T(8,128)}, f32[16,4,8,2,128]{4,2,3,1,0:T(8,128)S(1)}, u32[]{:S(2)}, u32[]{:S(2)}) collective-permute-start(f32[16,4,8,2,128]{4,2,3,1,0:T(8,128)} %reduce-scatter.2.cloned.1.call-done), channel_id=1, source_target_pairs={{0,16},{8,24},{16,32},{24,40},{32,48},{40,56},{48,64},{56,72},{64,... | collective-permute-start | bytes 1572872 | tf_op jit(solution)/shard_map/ppermute | solution.py:16
  157.0 21.6 %collective-permute-start.2 = (f32[16,4,8,2,128]{4,2,3,1,0:T(8,128)}, f32[16,4,8,2,128]{4,2,3,1,0:T(8,128)S(1)}, u32[]{:S(2)}, u32[]{:S(2)}) collective-permute-start(f32[16,4,8,2,128]{4,2,3,1,0:T(8,128)} %reduce-scatter.2.cloned.1.call-done), channel_id=1, source_target_pairs={{0,8},{8,16},{16,24},{24,32},{32,40},{40,48},{48,56},{56,64},{64,7... | collective-permute-start | bytes 1572872 | tf_op jit(solution)/shard_map/ppermute | solution.py:16
Sparse Core Ops, SparseCore 0:
  99.5 54.0 reduce-scatter.1
where the time goes:
time: 189 us; the launch traced here: 188 us
  waiting for transfers between devices  99.4 us (53%)
  local copies, waits for them, and re-layouts  35.9 us (19%)
  starting transfers between devices  16.1 us (9%)
  matrix products  14.7 us (8%)
  between operations  14.4 us (8%)
  other arithmetic  7.32 us (4%)
    reduce_scatter x1, waiting for transfers between devices, shards(): lax.psum_scatter(terms * weight[None, :, :, None, None], 'freq', scatter_...  54.2 us
    ppermute x4, waiting for transfers between devices, shifted(): lax.ppermute(value, axis, [(source, source + steps) for source in range(i...  45.2 us
    ppermute x4, starting transfers between devices, shifted(): lax.ppermute(value, axis, [(source, source + steps) for source in range(i...  16.1 us
    dot_general x8, matrix products, shards(): jnp.einsum('cbi,cbj->ibj', own, wide_twin[:, upper_k:upper_k + blocks_her...  9.82 us
    concatenate x1, local copies, waits for them, and re-layouts, turned_rows(): twin = jnp.concatenate([window[1:2], -window[0:1]], axis=0)  5.8 us
    concatenate x1, local copies, waits for them, and re-layouts, shards(): window = jnp.concatenate([masked] + ahead, axis=3)  5.77 us
    unnamed x30, local copies, waits for them, and re-layouts  5.61 us
    mul x1, local copies, waits for them, and re-layouts, shards(): terms * weight[None, :, :, None, None]  5.49 us
  transfers between devices with their start and end apart: 5, of which 5 were waited for; matrix products, arithmetic and copies ran while one was open for 3% of the time, Pallas kernels for 0%

commit v1 on v0

v1 whole, which is shorter than its diff:
```python
import math

import jax
import jax.numpy as jnp
from jax import lax
from jax.experimental import pallas as pl
from jax.experimental.pallas import tpu as pltpu
from jax.sharding import PartitionSpec as P

BINS = 2048
SEGS = 2
KOFF = 8
LANE = 128
OWN = 4
PREV = 3
KEEP = 16
HALVES = 2
RING = 4
EXTRA = 8
FULL = 32700.0
MID = 32768
SMALLEST = 1e-33
ON_MESH = pl.DeviceIdType.MESH

GROUPS = (
    ("x", ((0, 1, 3, 0), (1, 2, 4, 0), (2, 3, 5, 0))),
    ("y", ((3, 4, 6, 0),)),
    ("x", ((4, 4, 6, 1),)),
    ("y", ((5, 4, 6, 2),)),
    ("x", ((6, 4, 6, 3),)),
    ("y", ((4, 3, 2, 5), (5, 2, 2, 6), (6, 1, 2, 7))),
    ("x", ((7, 4, 6, 4),)),
)


def group_pairs(group):
    return sum(job[1] for job in group[1])


def packed(re, im):
    top = jnp.max(jnp.maximum(jnp.abs(re), jnp.abs(im)), axis=0, keepdims=True)
    power = jnp.ceil(jnp.log2(jnp.maximum(top, SMALLEST)))
    factor = FULL * jnp.exp2(-power)
    high = (re * factor + (MID + 0.5)).astype(jnp.int32)
    low = (im * factor + (MID + 0.5)).astype(jnp.int32)
    return lax.bitwise_or(lax.shift_left(high, jnp.full_like(high, 16)), low), power.astype(jnp.int32)


def unpacked(word, power):
    step = jnp.exp2(power.astype(jnp.float32)) * (1.0 / FULL)
    high = lax.shift_right_logical(word, jnp.full_like(word, 16)) - MID
    low = lax.bitwise_and(word, jnp.full_like(word, 65535)) - MID
    return high.astype(jnp.float32) * step, low.astype(jnp.float32) * step


def kernel(reach_ref, valid_ref, gap_ref, spectra_ref, upper_ref, lower_ref, *scratch):
    right, left, turned, weights, weights_prev, send_sem, recv_sem = scratch[:7]
    buffers = [scratch[7 + 6 * g : 13 + 6 * g] for g in range(len(GROUPS))]
    depth = spectra_ref.shape[0]
    half = depth // 2
    lanes = lax.axis_size("chan")
    chan = lax.axis_index("chan")
    freq = lax.axis_index("freq")
    x_own = freq // RING
    y_own = lax.rem(freq, RING)
    after = (lax.rem(chan + 1, lanes), freq)
    before = (lax.rem(chan + lanes - 1, lanes), freq)
    across = (chan, (1 - x_own) * RING + y_own)
    around = [(chan, x_own * RING + lax.rem(y_own + step, RING)) for step in range(1, RING)]

    barrier = pltpu.get_barrier_semaphore()
    for peer in [after, before, across] + around:
        pl.semaphore_signal(barrier, inc=1, device_id=peer, device_id_type=ON_MESH)

    count = [0]

    def remote(source, target, peer):
        slot = count[0]
        count[0] = slot + 1
        return pltpu.make_async_remote_copy(
            src_ref=source,
            dst_ref=target,
            send_sem=send_sem.at[slot],
            recv_sem=recv_sem.at[slot],
            device_id=peer,
            device_id_type=ON_MESH,
        )

    for b in range(OWN):
        live = gap_ref[b : b + 1, :].astype(jnp.float32).astype(jnp.bfloat16)
        right[b] = spectra_ref[:, b * LANE : (b + 1) * LANE] * live
    for i in range(OWN):
        for k in range(KOFF):
            keep = (k < reach_ref[i]) & (valid_ref[i, k] > 0) & (chan * OWN + i + k < lanes * OWN)
            value = jnp.where(keep, 1.0 / math.sqrt(SEGS * BINS), 0.0).astype(jnp.float32)
            weights[i * KOFF + k : i * KOFF + k + 1, :] = jnp.full((1, LANE), value, jnp.float32)

    pl.semaphore_wait(barrier, 6)
    send_right = [remote(right.at[b], right.at[OWN + b], before) for b in range(OWN)]
    for copy in send_right:
        copy.start()

    send_left = [remote(left.at[PREV + b], left.at[b - 1], after) for b in range(1, OWN)]
    for b in reversed(range(OWN)):
        for t in range(depth // LANE):
            tile = right[b, t * LANE : (t + 1) * LANE, :]
            turned[:, t * LANE : (t + 1) * LANE] = tile.T
        for hx in range(HALVES):
            for dy in range(RING):
                part = lax.rem(x_own + hx, HALVES) * RING + lax.rem(y_own + dy, RING)
                row = pl.multiple_of(part * KEEP, KEEP)
                to = (hx * RING + dy) * KEEP
                left[PREV + b, to : to + KEEP, :] = turned[pl.ds(row, KEEP), :]
        if b > 0:
            send_left[b - 1].start()
    send_weights = remote(weights, weights_prev, after)
    send_weights.start()

    first, second = [], []
    for (kind, _), (_, s1, r1, s2, r2, _) in zip(GROUPS, buffers):
        one_x = lambda s, r: [remote(s.at[0], r.at[0], across)]
        all_y = lambda s, r: [remote(s.at[d], r.at[d], around[d]) for d in range(RING - 1)]
        first.append(one_x(s1, r1) if kind == "x" else all_y(s1, r1))
        second.append(all_y(s2, r2) if kind == "x" else one_x(s2, r2))

    def put(ref, piece, rows, total, s, re, im):
        word, power = packed(re, im)
        ref[piece, pl.ds(pl.multiple_of(s * rows, rows), rows), :] = word
        ref[piece, pl.ds(total * rows + s, 1), :] = power

    def take(ref, piece, rows, total, s):
        word = ref[piece, pl.ds(pl.multiple_of(s * rows, rows), rows), :]
        return unpacked(word, ref[piece, pl.ds(total * rows + s, 1), :])

    def compute(g):
        kind, jobs = GROUPS[g]
        total = group_pairs(GROUPS[g])
        acc, s1 = buffers[g][0], buffers[g][1]
        side = HALVES * KEEP
        base = 0
        for column, pairs, row, _ in jobs:

            def step(n, carry, column=column, row=row, base=base):
                s = base + n
                a = left[row - n]
                re = jnp.dot(a, right[column], preferred_element_type=jnp.float32)
                im = jnp.dot(a[:, :half], right[column, half:], preferred_element_type=jnp.float32)
                im = im - jnp.dot(a[:, half:], right[column, :half], preferred_element_type=jnp.float32)
                if kind == "x":
                    span = RING * KEEP
                    acc[s, 0] = re[:span]
                    acc[s, 1] = im[:span]
                    put(s1, 0, span, total, s, re[span:], im[span:])
                else:
                    for dy in range(RING):
                        low, high = dy * KEEP, (RING + dy) * KEEP
                        re_part = jnp.concatenate([re[low : low + KEEP], re[high : high + KEEP]], axis=0)
                        im_part = jnp.concatenate([im[low : low + KEEP], im[high : high + KEEP]], axis=0)
                        if dy == 0:
                            acc[s, 0] = re_part
                            acc[s, 1] = im_part
                        else:
                            put(s1, dy - 1, side, total, s, re_part, im_part)
                return carry

            lax.fori_loop(0, pairs, step, 0)
            base += pairs
        for copy in first[g]:
            copy.start()

    def middle(g):
        kind, _ = GROUPS[g]
        total = group_pairs(GROUPS[g])
        acc, _, r1, s2 = buffers[g][:4]
        for copy in first[g]:
            copy.wait_recv()

        def step(s, carry):
            re, im = acc[s, 0], acc[s, 1]
            for piece in range(len(first[g])):
                more_re, more_im = take(r1, piece, re.shape[0], total, s)
                re, im = re + more_re, im + more_im
            acc[s, 0, :KEEP] = re[:KEEP]
            acc[s, 1, :KEEP] = im[:KEEP]
            for piece in range(len(second[g])):
                rows = slice((piece + 1) * KEEP, (piece + 2) * KEEP)
                put(s2, piece, KEEP, total, s, re[rows], im[rows])
            return carry

        lax.fori_loop(0, total, step, 0)
        for copy in second[g]:
            copy.start()

    outgoing = []

    def finish(g):
        _, jobs = GROUPS[g]
        total = group_pairs(GROUPS[g])
        acc, r2, done = buffers[g][0], buffers[g][4], buffers[g][5]
        for copy in second[g]:
            copy.wait_recv()
        s = 0
        for column, pairs, row, offset in jobs:
            start = s
            for n in range(pairs):
                i, k = row - n - PREV, offset + n
                re, im = acc[s, 0, :KEEP], acc[s, 1, :KEEP]
                for piece in range(len(second[g])):
                    more_re, more_im = take(r2, piece, KEEP, total, s)
                    re, im = re + more_re, im + more_im
                at = (i % OWN) * KOFF + k
                scale = (weights if i >= 0 else weights_prev)[at : at + 1, :]
                re, im = re * scale, im * scale
                if i >= 0:
                    upper_ref[at, 0] = re
                    upper_ref[at, 1] = im
                if column < OWN:
                    lower_ref[column * KOFF + k, 0] = re
                    lower_ref[column * KOFF + k, 1] = im
                else:
                    done[s, 0] = re
                    done[s, 1] = im
                if i < 0:
                    outgoing.append(remote(done.at[s], upper_ref.at[at], before))
                s += 1
            if column >= OWN:
                at = (column - OWN) * KOFF + offset
                outgoing.append(remote(done.at[pl.ds(start, pairs)], lower_ref.at[pl.ds(at, pairs)], after))
        return

    started = [0]

    def launch():
        for copy in outgoing[started[0] :]:
            copy.start()
        started[0] = len(outgoing)

    compute(0)
    compute(1)
    send_right[0].wait_recv()
    compute(2)
    middle(0)
    send_right[1].wait_recv()
    compute(3)
    middle(1)
    finish(0)
    send_right[2].wait_recv()
    compute(4)
    middle(2)
    finish(1)
    for copy in send_left:
        copy.wait_recv()
    compute(5)
    middle(3)
    finish(2)
    launch()
    send_right[3].wait_recv()
    compute(6)
    middle(4)
    finish(3)
    launch()
    middle(5)
    finish(4)
    launch()
    middle(6)
    send_weights.wait_recv()
    finish(5)
    launch()
    finish(6)
    launch()
    for copy in outgoing:
        copy.wait_recv()
    for copy in send_right + send_left + [send_weights] + sum(first, []) + sum(second, []) + outgoing:
        copy.wait_send()


def scratch_shapes(depth):
    shapes = [
        pltpu.VMEM((2 * OWN, depth, LANE), jnp.bfloat16),
        pltpu.VMEM((PREV + OWN, LANE, depth), jnp.bfloat16),
        pltpu.VMEM((LANE, depth), jnp.bfloat16),
        pltpu.VMEM((OWN * KOFF, LANE), jnp.float32),
        pltpu.VMEM((OWN * KOFF, LANE), jnp.float32),
        pltpu.SemaphoreType.DMA((64,)),
        pltpu.SemaphoreType.DMA((64,)),
    ]
    for group in GROUPS:
        total = group_pairs(group)
        wide = RING if group[0] == "x" else HALVES
        one = lambda rows: pltpu.VMEM((1, total * rows + EXTRA, LANE), jnp.int32)
        three = lambda rows: pltpu.VMEM((RING - 1, total * rows + EXTRA, LANE), jnp.int32)
        s1 = (one if group[0] == "x" else three)(wide * KEEP)
        s2 = (three if group[0] == "x" else one)(KEEP)
        shapes += [
            pltpu.VMEM((total, 2, wide * KEEP, LANE), jnp.float32),
            s1,
            s1,
            s2,
            s2,
            pltpu.VMEM((total, 2, KEEP, LANE), jnp.float32),
        ]
    return shapes


def shards(spectra, gap, reach, valid):
    depth = spectra.shape[0] * spectra.shape[1] * spectra.shape[2]
    flat = spectra.reshape(depth, spectra.shape[3])
    pairs = OWN * KOFF
    result = jax.ShapeDtypeStruct((pairs, 2, KEEP, LANE), jnp.float32)
    in_vmem = pl.BlockSpec(memory_space=pltpu.VMEM)
    in_smem = pl.BlockSpec(memory_space=pltpu.SMEM)
    upper, lower = pl.pallas_call(
        kernel,
        out_shape=(result, result),
        in_specs=[in_smem, in_smem, in_vmem, in_vmem],
        out_specs=(in_vmem, in_vmem),
        scratch_shapes=scratch_shapes(depth),
        compiler_params=pltpu.CompilerParams(
            collective_id=0, has_side_effects=True, vmem_limit_bytes=40 * 2**20
        ),
        cost_estimate=pl.CostEstimate(flops=4 * pairs * depth * LANE * LANE, bytes_accessed=2**21, transcendentals=0),
        name="spectral_pairs",
    )(reach, valid, gap.reshape(OWN, LANE), flat)
    order = (3, 0, 1, 2, 4)
    sign = jnp.array([1.0, -1.0], dtype=jnp.float32)
    upper = upper.reshape(OWN, KOFF, 2, KEEP, LANE).transpose(order)
    lower = lower.reshape(OWN, KOFF, 2, KEEP, LANE).transpose(order)
    return upper, lower * sign[None, None, None, :, None]


def solution(mesh):
    placed = (P(None, None, "freq", "chan"), P("chan"), P("chan"), P("chan", None))
    return jax.shard_map(
        shards,
        mesh=mesh,
        in_specs=placed,
        out_specs=(P("freq", "chan", None, None, None), P("freq", "chan", None, None, None)),
        check_vma=False,
    )
```

time: 189 us -> 57.7 us (0.31)
  waiting for transfers between devices: 99.4 us -> 0 us
  Pallas kernels: 0 us -> 50.7 us
  local copies, waits for them, and re-layouts: 35.9 us -> 5.36 us
  starting transfers between devices: 16.1 us -> 0 us
  matrix products: 14.7 us -> 0 us
  between operations: 14.4 us -> 0.67 us
  other arithmetic: 7.32 us -> 0.12 us
    reduce_scatter x1 -> x0, waiting for transfers between devices: 54.2 us -> none  [shards(): lax.psum_scatter(terms * weight[None, :, :, None, None], 'freq', scatter_...]
    pallas_call x0 -> x1, Pallas kernels: none -> 50.7 us  [shards(): pl.pallas_call(kernel, out_shape=(result, result), in_specs=[in_smem, in_...]
    ppermute x4 -> x0, waiting for transfers between devices: 45.2 us -> none  [shifted(): lax.ppermute(value, axis, [(source, source + steps) for source in range(i...]
    ppermute x4 -> x0, starting transfers between devices: 16.1 us -> none  [shifted(): lax.ppermute(value, axis, [(source, source + steps) for source in range(i...]
    dot_general x16 -> x0, matrix products: 14.7 us -> none  [the longest x8 9.82 us: shards(): jnp.einsum('cbi,cbj->ibj', own, wide_twin[:, upper_k:upper_k + blocks_her...]
    concatenate x2 -> x0, local copies, waits for them, and re-layouts: 11.6 us -> none  [the longest x1 5.8 us: turned_rows(): twin = jnp.concatenate([window[1:2], -window[0:1]], axis=0)]
    reshape x3 -> x1, local copies, waits for them, and re-layouts: 10.5 us -> 1.06 us  [shards(): upper = upper.reshape(OWN, KOFF, 2, KEEP, LANE).transpose(order)]
    mul x1 -> x0, local copies, waits for them, and re-layouts: 5.49 us -> none  [shards(): terms * weight[None, :, :, None, None]]
  transfers between devices with their start and end apart: 5 -> 0, of which waited for: 5 -> 0; matrix products, arithmetic and copies ran while one was open for 3% -> 0% of each run, Pallas kernels for 0% -> 0%
where the time goes in v1:
time: 57.7 us; the launch traced here: 56.8 us
  Pallas kernels  50.7 us (88%)
  local copies, waits for them, and re-layouts  5.36 us (9%)
  between operations  0.67 us (1%)
    pallas_call x1, Pallas kernels, shards(): pl.pallas_call(kernel, out_shape=(result, result), in_specs=[in_smem, in_...  50.7 us
    unnamed x11, local copies, waits for them, and re-layouts  4.3 us

profile of v1, /device:TPU:6, one launch (start us, length us, event | category | flops | bytes accessed | tf_op | source)
XLA Modules:
  0.0 56.8 jit_solution(7269403439597504772)
XLA Ops:
  0.6 0.0 copy-start.1
  0.6 0.0 copy-start.3
  0.7 0.7 %copy-done.1 = s32[4,8]{1,0:T(4,128)S(1)} copy-done((s32[4,8]{1,0:T(4,128)S(1)}, s32[4,8]{1,0:T(4,128)}, u32[]{:S(2)}) %copy-start.1) | copy-done | bytes 152
  1.3 0.0 copy-done.3
  1.3 0.0 copy-start
  1.3 1.2 %copy-done = bf16[2,2,256,512]{3,2,1,0:T(8,128)(2,1)S(1)} copy-done((bf16[2,2,256,512]{3,2,1,0:T(8,128)(2,1)S(1)}, bf16[2,2,256,512]{3,2,1,0:T(8,128)(2,1)}, u32[]{:S(2)}) %copy-start) | copy-done | bytes 1048600
  2.5 0.0 copy-start.2
  2.5 0.7 %copy-done.2 = s32[512]{0:T(512)S(1)} copy-done((s32[512]{0:T(512)S(1)}, s32[512]{0:T(512)}, u32[]{:S(2)}) %copy-start.2) | copy-done | bytes 2072
  3.2 50.7 %spectral_pairs.1 = (f32[32,2,16,128]{3,2,1,0:T(8,128)S(1)}, f32[32,2,16,128]{3,2,1,0:T(8,128)S(1)}) custom-call(s32[4]{0:T(128)S(1)} %copy-done.3, s32[4,8]{1,0:T(4,128)S(1)} %copy-done.1, s32[4,128]{1,0:T(4,128)S(1)} %bitcast.12, bf16[1024,512]{1,0:T(8,128)(2,1)S(1)} %bitcast.11), custom_call_target="tpu_custom_call" | custom-call | flops 2147483648 | bytes 2097152 | tf_op jit(solution)/shard_map/spectral_pairs/pallas_call | solution.py:312
  53.9 1.1 %copy.12 = f32[4,8,2,16,128]{4,2,1,0,3:T(2,128)} copy(f32[4,8,2,16,128]{4,3,2,1,0:T(8,128)S(1)} %bitcast.9) | data formatting | bytes 1048576 | tf_op jit(solution)/shard_map/reshape | solution.py:326
  55.0 0.0 copy-start.4
  55.0 0.7 %copy-done.4 = f32[2]{0:T(128)S(1)} copy-done((f32[2]{0:T(128)S(1)}, f32[2]{0:T(128)}, u32[]{:S(2)}) %copy-start.4) | copy-done | bytes 32
  55.6 0.1 multiply_bitcast_fusion
  55.8 1.1 %copy.10 = f32[16,4,8,2,128]{4,3,2,1,0:T(2,128)} copy(f32[16,4,8,2,128]{4,0,3,2,1:T(8,128)S(1)} %multiply_bitcast_fusion) | data formatting | bytes 1048576
Async XLA Ops:
  0.6 0.7 %copy-start.1 = (s32[4,8]{1,0:T(4,128)S(1)}, s32[4,8]{1,0:T(4,128)}, u32[]{:S(2)}) copy-start(s32[4,8]{1,0:T(4,128)} %valid_ref.1) | copy-start | bytes 388
  0.6 0.7 %copy-start.3 = (s32[4]{0:T(128)S(1)}, s32[4]{0:T(128)}, u32[]{:S(2)}) copy-start(s32[4]{0:T(128)} %reach_ref.1) | copy-start | bytes 52
  1.3 1.2 %copy-start = (bf16[2,2,256,512]{3,2,1,0:T(8,128)(2,1)S(1)}, bf16[2,2,256,512]{3,2,1,0:T(8,128)(2,1)}, u32[]{:S(2)}) copy-start(bf16[2,2,256,512]{3,2,1,0:T(8,128)(2,1)} %param.5) | copy-start | bytes 3145732
  2.5 0.7 %copy-start.2 = (s32[512]{0:T(512)S(1)}, s32[512]{0:T(512)}, u32[]{:S(2)}) copy-start(s32[512]{0:T(512)} %param.6) | copy-start | bytes 6148
  55.0 0.7 %copy-start.4 = (f32[2]{0:T(128)S(1)}, f32[2]{0:T(128)}, u32[]{:S(2)}) copy-start(f32[2]{0:T(128)} %constant.2.clone) | copy-start | bytes 28

commit v2 on v0

v2 whole, which is shorter than its diff:
```python
import math

import jax
import jax.numpy as jnp
from jax import lax
from jax.experimental import pallas as pl
from jax.experimental.pallas import tpu as pltpu
from jax.sharding import PartitionSpec as P

BINS = 2048
SEGS = 2
KOFF = 8
LANE = 128
OWN = 4
PREV = 3
KEEP = 16
RING = 4
SHARES = 8
POWERS = 4
FULL = 32700.0
MID = 32768
SMALLEST = 1e-33
ON_MESH = pl.DeviceIdType.MESH

FLIPS = {"x": 4, "b": 2, "a": 1}
OWN_FIRST = ((0, 1, 3, 0), (1, 2, 4, 0), (2, 3, 5, 0))
OWN_LAST = ((3, 4, 6, 0),)
EVEN = (
    (("b", "x", "a"), OWN_FIRST),
    (("a", "b", "x"), OWN_LAST),
    (("b", "a", "x"), ((4, 4, 6, 1),)),
    (("b", "x", "a"), ((5, 4, 6, 2),)),
    (("a", "b", "x"), ((6, 4, 6, 3),)),
    (("b", "a", "x"), ((7, 4, 6, 4),)),
    (("a", "x", "b"), ((4, 1, 2, 5), (5, 1, 2, 6), (6, 1, 2, 7))),
    (("b", "xa"), ((4, 2, 1, 6), (5, 1, 1, 7))),
)
ODD = (
    (("b", "a", "x"), OWN_FIRST),
    (("a", "x", "b"), OWN_LAST),
    (("a", "xb"), ((4, 7, 6, 1),)),
    (("x", "ab"), ((5, 6, 6, 2),)),
    (("a", "xb"), ((6, 5, 6, 3),)),
    (("b", "xa"), ((7, 4, 6, 4),)),
)
EVEN_STEPS = (
    "c0", "c1", "a4", "w", "c2", "a5", "c3", "a6", "c4", "a7", "c5", "p2", "c6", "m1.1", "m0.1", "m4.1",
    "m2.1", "p1", "p0", "c7", "m3.1", "m6.1", "m5.1", "m0.2", "m1.2", "m2.2", "m4.2", "m3.2", "m6.2", "m7.1", "m5.2", "f1",
    "f0", "f2", "f3", "f4", "v", "f6", "f7", "f5",
)
ODD_STEPS = (
    "c0", "c1", "p2", "p1", "p0", "a4", "w", "c2", "m1.1", "a5", "c3", "m0.1", "m1.2", "a6", "c4", "m2.1",
    "a7", "c5", "m0.2", "f1", "m3.1", "m4.1", "v", "f2", "m5.1", "f0", "f3", "f4", "f5",
)


def group_pairs(group):
    return sum(job[1] for job in group[1])


def group_phases(group):
    phases, chunks = [], SHARES
    for flips in group[0]:
        pieces = 2 ** len(flips)
        chunks //= pieces
        masks = [
            sum(FLIPS[name] for bit, name in enumerate(reversed(flips)) if piece >> bit & 1)
            for piece in range(pieces)
        ]
        phases.append((masks[1:], chunks))
    return phases


def group_order(group):
    names = "".join(group[0])[::-1]
    return [sum(FLIPS[name] for bit, name in enumerate(names) if at >> bit & 1) for at in range(SHARES)]


def packed(re, im):
    top = jnp.max(jnp.maximum(jnp.abs(re), jnp.abs(im)), axis=0, keepdims=True)
    power = jnp.ceil(jnp.log2(jnp.maximum(top, SMALLEST)))
    factor = FULL * jnp.exp2(-power)
    high = (re * factor + (MID + 0.5)).astype(jnp.int32)
    low = (im * factor + (MID + 0.5)).astype(jnp.int32)
    return lax.bitwise_or(lax.shift_left(high, jnp.full_like(high, 16)), low), power.astype(jnp.int32)


def unpacked(word, power):
    step = jnp.exp2(power.astype(jnp.float32)) * (1.0 / FULL)
    high = lax.shift_right_logical(word, jnp.full_like(word, 16)) - MID
    low = lax.bitwise_and(word, jnp.full_like(word, 65535)) - MID
    return high.astype(jnp.float32) * step, low.astype(jnp.float32) * step


class Plan:
    def __init__(self, groups, scratch, remote, peers):
        self.groups = groups
        self.acc, self.done, self.sent, self.got, self.sums = [], [], [], [], []
        rest = list(scratch)
        for group in groups:
            self.acc.append(rest.pop(0))
            self.done.append(rest.pop(0))
            self.sent.append([rest.pop(0) for _ in group[0]])
            self.got.append([rest.pop(0) for _ in group[0]])
            self.sums.append(
                [
                    [remote(sent.at[n], got.at[n], peers[mask]) for n, mask in enumerate(masks)]
                    for sent, got, (masks, _) in zip(self.sent[-1], self.got[-1], group_phases(group))
                ]
            )
        self.buffers = len(scratch) - len(rest)

    def exchange(self, remote, upper_ref, lower_ref, before, after):
        self.outgoing = []
        for group, done in zip(self.groups, self.done):
            total, s, copies = group_pairs(group), 0, []
            for column, pairs, row, offset in group[1]:
                for n in range(pairs):
                    if row - n < PREV:
                        at = (row - n + 1) * KOFF + offset + n
                        copies.append(remote(done.at[total + s + n], upper_ref.at[at], before))
                if column >= OWN:
                    at = (column - OWN) * KOFF + offset
                    copies.append(remote(done.at[pl.ds(s, pairs)], lower_ref.at[pl.ds(at, pairs)], after))
                s += pairs
            self.outgoing.append(copies)


class Guarded:
    def __init__(self, copy, sends, receives):
        self.copy, self.sends, self.receives = copy, sends, receives

    def start(self):
        pl.when(self.sends)(self.copy.start)

    def wait_send(self):
        pl.when(self.sends)(self.copy.wait_send)

    def wait_recv(self):
        pl.when(self.receives)(self.copy.wait_recv)


def kernel(reach_ref, valid_ref, gap_ref, spectra_ref, upper_ref, lower_ref, *scratch):
    staged, live, reach, valid, wide, left, turned, products, weights, weights_prev = scratch[:10]
    load_sem, send_sem, recv_sem = scratch[10:13]
    depth = spectra_ref.shape[0]
    half = depth // 2
    lanes = lax.axis_size("chan")
    chan = lax.axis_index("chan")
    freq = lax.axis_index("freq")
    x_own = freq // RING
    y_own = lax.rem(freq, RING)
    after = (lax.rem(chan + 1, lanes), freq)
    before = (lax.rem(chan + lanes - 1, lanes), freq)
    y_by_flips = [y_own, y_own + 1 - 2 * lax.rem(y_own, 2), RING - 1 - y_own, lax.rem(y_own + 2, RING)]
    places = [lax.rem(x_own + mask // RING, 2) * RING + y_by_flips[mask % RING] for mask in range(SHARES)]
    peers = [(chan, place) for place in places]
    has_after = chan < lanes - 1
    has_before = chan > 0

    barrier = pltpu.get_barrier_semaphore()
    for peer in [after, before] + peers[1:]:
        pl.semaphore_signal(barrier, inc=1, device_id=peer, device_id_type=ON_MESH)

    def column(b):
        return spectra_ref.at[:, pl.ds(b * LANE, LANE)]

    loads = [pltpu.make_async_copy(column(b), staged.at[b], load_sem.at[b]) for b in range(OWN)]
    loads.append(pltpu.make_async_copy(gap_ref, live.at[0], load_sem.at[OWN]))
    loads.append(pltpu.make_async_copy(reach_ref, reach, load_sem.at[OWN + 1]))
    loads.append(pltpu.make_async_copy(valid_ref, valid, load_sem.at[OWN + 2]))
    for copy in loads:
        copy.start()

    count = [0]

    def remote(source, target, peer):
        slot = count[0]
        count[0] = slot + 1
        copy = pltpu.make_async_remote_copy(
            src_ref=source,
            dst_ref=target,
            send_sem=send_sem.at[slot],
            recv_sem=recv_sem.at[slot],
            device_id=peer,
            device_id_type=ON_MESH,
        )
        if peer is after:
            return Guarded(copy, has_after, has_before)
        if peer is before:
            return Guarded(copy, has_before, has_after)
        return copy

    send_live = [remote(gap_ref, live.at[1], before), remote(gap_ref, live.at[2], after)]
    send_right = [remote(column(b), staged.at[OWN + b], before) for b in range(OWN)]
    send_left = [remote(column(b), staged.at[2 * OWN + b - 1], after) for b in range(1, OWN)]

    pl.semaphore_wait(barrier, 2 + len(peers) - 1)
    for copy in send_live + send_right + send_left[::-1]:
        copy.start()

    @pl.when(chan == lanes - 1)
    def _():
        live[1] = jnp.zeros_like(live[1])
        staged[OWN : 2 * OWN] = jnp.zeros_like(staged[OWN : 2 * OWN])
        for i in range(1, OWN):
            for k in range(KOFF - i, KOFF):
                upper_ref[i * KOFF + k] = jnp.zeros_like(upper_ref[0])

    @pl.when(chan == 0)
    def _():
        live[2] = jnp.zeros_like(live[2])
        staged[2 * OWN :] = jnp.zeros_like(staged[2 * OWN :])
        weights_prev[...] = jnp.zeros_like(weights_prev)
        for j in range(OWN):
            for k in range(j + 1, KOFF):
                lower_ref[j * KOFF + k] = jnp.zeros_like(lower_ref[0])

    def masked(slot, side, b):
        return staged[slot] * live[side, b : b + 1, :].astype(jnp.float32).astype(jnp.bfloat16)

    def widen(b, block):
        wide[b, :, :LANE] = block
        wide[b, :half, LANE:] = block[half:]
        wide[b, half:, LANE:] = -block[:half]

    def turn(row, block):
        for t in range(depth // LANE):
            turned[:, t * LANE : (t + 1) * LANE] = block[t * LANE : (t + 1) * LANE].T
        for mask in range(SHARES):
            at = pl.multiple_of(places[mask] * KEEP, KEEP)
            left[row, mask * KEEP : (mask + 1) * KEEP, :] = turned[pl.ds(at, KEEP), :]

    loads[OWN].wait()
    for b in range(OWN):
        loads[b].wait()
        block = masked(b, 0, b)
        widen(b, block)
        turn(PREV + b, block)

    send_weights = remote(weights, weights_prev, after)

    def weigh():
        loads[OWN + 1].wait()
        loads[OWN + 2].wait()
        for i in range(OWN):
            for k in range(KOFF):
                keep = (k < reach[i]) & (valid[i, k] > 0) & (chan * OWN + i + k < lanes * OWN)
                value = jnp.where(keep, 1.0 / math.sqrt(SEGS * BINS), 0.0).astype(jnp.float32)
                weights[i * KOFF + k : i * KOFF + k + 1, :] = jnp.full((1, LANE), value, jnp.float32)
        send_weights.start()

    def clear(plan, g, phase):
        total = group_pairs(plan.groups[g])
        masks, chunks = group_phases(plan.groups[g])[phase]
        for n in range(len(masks)):
            low, high = total * chunks * KEEP, plan.sent[g][phase].shape[1]
            plan.sent[g][phase][n, low:high, :] = jnp.zeros((high - low, LANE), jnp.int32)

    def put(ref, piece, rows, total, s, re, im):
        word, power = packed(re, im)
        ref[piece, pl.ds(pl.multiple_of(s * rows, rows), rows), :] = word
        at = pl.ds(total * rows + s // POWERS, 1)
        field = lax.shift_left(power + 128, jnp.full_like(power, 8 * lax.rem(s, POWERS)))
        ref[piece, at, :] = lax.bitwise_or(ref[piece, at, :], field)

    def take(ref, piece, rows, total, s):
        word = ref[piece, pl.ds(pl.multiple_of(s * rows, rows), rows), :]
        field = ref[piece, pl.ds(total * rows + s // POWERS, 1), :]
        field = lax.shift_right_logical(field, jnp.full_like(field, 8 * lax.rem(s, POWERS)))
        return unpacked(word, lax.bitwise_and(field, jnp.full_like(field, 255)) - 128)

    even = Plan(EVEN, scratch[13:], remote, peers)
    odd = Plan(ODD, scratch[13 + even.buffers :], remote, peers)
    even.exchange(remote, upper_ref, lower_ref, before, after)
    odd.exchange(remote, upper_ref, lower_ref, before, after)

    def run(plan, other, steps):
        def spread(g, phase, s, piece):
            total = group_pairs(plan.groups[g])
            masks, chunks = group_phases(plan.groups[g])[phase]
            rows = chunks * KEEP
            re, im = piece(0, chunks)
            plan.acc[g][s, 0, :rows] = re
            plan.acc[g][s, 1, :rows] = im
            for n in range(len(masks)):
                re, im = piece((n + 1) * chunks, (n + 2) * chunks)
                put(plan.sent[g][phase], n, rows, total, s, re, im)

        def gathered(g, phase, s):
            total = group_pairs(plan.groups[g])
            masks, chunks = group_phases(plan.groups[g])[phase]
            rows = chunks * KEEP
            re, im = plan.acc[g][s, 0, :rows], plan.acc[g][s, 1, :rows]
            for n in range(len(masks)):
                more_re, more_im = take(plan.got[g][phase], n, rows, total, s)
                re, im = re + more_re, im + more_im
            return re, im

        def compute(g):
            order = group_order(plan.groups[g])
            clear(plan, g, 0)
            base = 0
            for column, pairs, row, _ in plan.groups[g][1]:
                rows = left[row - pairs + 1 : row + 1].reshape(pairs * LANE, depth)
                products[: pairs * LANE] = jnp.dot(rows, wide[column], preferred_element_type=jnp.float32)

                def step(n, carry, pairs=pairs, base=base):
                    at = (pairs - 1 - n) * LANE

                    def piece(low, high):
                        parts = [
                            products[pl.ds(pl.multiple_of(at + order[p] * KEEP, KEEP), KEEP), :] for p in range(low, high)
                        ]
                        both = jnp.concatenate(parts, axis=0)
                        return both[:, :LANE], both[:, LANE:]

                    spread(g, 0, n + base, piece)
                    return carry

                lax.fori_loop(0, pairs, step, 0, unroll=True)
                base += pairs
            for copy in plan.sums[g][0]:
                copy.start()

        def middle(g, phase):
            clear(plan, g, phase)
            for copy in plan.sums[g][phase - 1]:
                copy.wait_recv()

            def step(s, carry):
                re, im = gathered(g, phase - 1, s)
                spread(g, phase, s, lambda low, high: (re[low * KEEP : high * KEEP], im[low * KEEP : high * KEEP]))
                return carry

            lax.fori_loop(0, group_pairs(plan.groups[g]), step, 0, unroll=True)
            for copy in plan.sums[g][phase]:
                copy.start()

        def finish(g):
            _, jobs = plan.groups[g]
            total = group_pairs(plan.groups[g])
            phase = len(plan.sums[g]) - 1
            for copy in plan.sums[g][phase]:
                copy.wait_recv()
            s = 0
            for column, pairs, row, offset in jobs:
                for n in range(pairs):
                    i, k = row - n - PREV, offset + n
                    re, im = gathered(g, phase, s)
                    at = (i % OWN) * KOFF + k
                    scale = (weights if i >= 0 else weights_prev)[at : at + 1, :]
                    re, im = re * scale, im * scale
                    if i >= 0:
                        upper_ref[at, 0] = re
                        upper_ref[at, 1] = im
                    if column < OWN:
                        lower_ref[column * KOFF + k, 0] = re
                        lower_ref[column * KOFF + k, 1] = -im
                    else:
                        plan.done[g][s, 0] = re
                        plan.done[g][s, 1] = -im
                    if i < 0:
                        plan.done[g][total + s, 0] = re
                        plan.done[g][total + s, 1] = im
                    s += 1
            for copy in plan.outgoing[g]:
                copy.start()

        def arrive(b):
            if b == OWN:
                send_live[0].wait_recv()
            send_right[b - OWN].wait_recv()
            widen(b, masked(b, 1, b - OWN))

        def precede(row):
            if row == PREV - 1:
                send_live[1].wait_recv()
            send_left[row].wait_recv()
            turn(row, masked(2 * OWN + row, 2, row + 1))

        for name in steps:
            numbers = [int(part) for part in name[1:].split(".") if part]
            {
                "a": arrive,
                "p": precede,
                "c": compute,
                "m": middle,
                "f": finish,
                "w": weigh,
                "v": send_weights.wait_recv,
            }[name[0]](*numbers)
        for group in other.outgoing:
            for copy in group:
                copy.wait_recv()
        for group in plan.outgoing:
            for copy in group:
                copy.wait_send()
        for group in plan.sums:
            for phase in group:
                for copy in phase:
                    copy.wait_send()

    @pl.when(lax.rem(chan, 2) == 0)
    def _():
        run(even, odd, EVEN_STEPS)

    @pl.when(lax.rem(chan, 2) == 1)
    def _():
        run(odd, even, ODD_STEPS)

    for copy in send_live + send_right + send_left + [send_weights]:
        copy.wait_send()


def scratch_shapes(depth):
    shapes = [
        pltpu.VMEM((2 * OWN + PREV, depth, LANE), jnp.bfloat16),
        pltpu.VMEM((3, OWN, LANE), jnp.int32),
        pltpu.SMEM((OWN,), jnp.int32),
        pltpu.SMEM((OWN, KOFF), jnp.int32),
        pltpu.VMEM((2 * OWN, depth, 2 * LANE), jnp.bfloat16),
        pltpu.VMEM((PREV + OWN, LANE, depth), jnp.bfloat16),
        pltpu.VMEM((LANE, depth), jnp.bfloat16),
        pltpu.VMEM(((OWN + PREV) * LANE, 2 * LANE), jnp.float32),
        pltpu.VMEM((OWN * KOFF, LANE), jnp.float32),
        pltpu.VMEM((OWN * KOFF, LANE), jnp.float32),
        pltpu.SemaphoreType.DMA((OWN + 3,)),
        pltpu.SemaphoreType.DMA((128,)),
        pltpu.SemaphoreType.DMA((128,)),
    ]
    for group in EVEN + ODD:
        total = group_pairs(group)
        phases = group_phases(group)
        moved = [
            pltpu.VMEM((len(masks), total * chunks * KEEP + pl.cdiv(total, POWERS), LANE), jnp.int32)
            for masks, chunks in phases
        ]
        shapes.append(pltpu.VMEM((total, 2, phases[0][1] * KEEP, LANE), jnp.float32))
        shapes.append(pltpu.VMEM((2 * total, 2, KEEP, LANE), jnp.float32))
        shapes += moved + moved
    return shapes


def shards(spectra, gap, reach, valid):
    depth = spectra.shape[0] * spectra.shape[1] * spectra.shape[2]
    flat = spectra.reshape(depth, spectra.shape[3])
    pairs = OWN * KOFF
    result = jax.ShapeDtypeStruct((pairs, 2, KEEP, LANE), jnp.float32)
    in_vmem = pl.BlockSpec(memory_space=pltpu.VMEM)
    anywhere = pl.BlockSpec(memory_space=pl.ANY)
    upper, lower = pl.pallas_call(
        kernel,
        out_shape=(result, result),
        in_specs=[anywhere] * 4,
        out_specs=(in_vmem, in_vmem),
        scratch_shapes=scratch_shapes(depth),
        compiler_params=pltpu.CompilerParams(
            collective_id=0, has_side_effects=True, vmem_limit_bytes=209 * 2**18
        ),
        cost_estimate=pl.CostEstimate(flops=4 * pairs * depth * LANE * LANE, bytes_accessed=2**21, transcendentals=0),
        name="spectral_pairs",
    )(*(pltpu.with_memory_space_constraint(a, pltpu.HBM) for a in (reach, valid, gap.reshape(OWN, LANE), flat)))
    order = (3, 0, 1, 2, 4)
    upper = upper.reshape(OWN, KOFF, 2, KEEP, LANE).transpose(order)
    lower = lower.reshape(OWN, KOFF, 2, KEEP, LANE).transpose(order)
    return upper, lower


def solution(mesh):
    placed = (P(None, None, "freq", "chan"), P("chan"), P("chan"), P("chan", None))
    return jax.shard_map(
        shards,
        mesh=mesh,
        in_specs=placed,
        out_specs=(P("freq", "chan", None, None, None), P("freq", "chan", None, None, None)),
        check_vma=False,
    )
```

time: 189 us -> 41.2 us (0.22)
  waiting for transfers between devices: 99.4 us -> 0 us
  Pallas kernels: 0 us -> 38.9 us
  local copies, waits for them, and re-layouts: 35.9 us -> 1.51 us
  starting transfers between devices: 16.1 us -> 0 us
  matrix products: 14.7 us -> 0 us
  between operations: 14.4 us -> 0.64 us
  other arithmetic: 7.32 us -> 0 us
    reduce_scatter x1 -> x0, waiting for transfers between devices: 54.2 us -> none  [shards(): lax.psum_scatter(terms * weight[None, :, :, None, None], 'freq', scatter_...]
    ppermute x4 -> x0, waiting for transfers between devices: 45.2 us -> none  [shifted(): lax.ppermute(value, axis, [(source, source + steps) for source in range(i...]
    pallas_call x0 -> x1, Pallas kernels: none -> 38.9 us  [shards(): pl.pallas_call(kernel, out_shape=(result, result), in_specs=[anywhere] *...]
    ppermute x4 -> x0, starting transfers between devices: 16.1 us -> none  [shifted(): lax.ppermute(value, axis, [(source, source + steps) for source in range(i...]
    dot_general x16 -> x0, matrix products: 14.7 us -> none  [the longest x8 9.82 us: shards(): jnp.einsum('cbi,cbj->ibj', own, wide_twin[:, upper_k:upper_k + blocks_her...]
    concatenate x2 -> x0, local copies, waits for them, and re-layouts: 11.6 us -> none  [the longest x1 5.8 us: turned_rows(): twin = jnp.concatenate([window[1:2], -window[0:1]], axis=0)]
    reshape x3 -> x0, local copies, waits for them, and re-layouts: 10.5 us -> none  [the longest x1 4.68 us: turned_rows(): return twin.reshape(depth, count, width)]
    unnamed x30 -> x0, local copies, waits for them, and re-layouts: 5.61 us -> none
  transfers between devices with their start and end apart: 5 -> 0, of which waited for: 5 -> 0; matrix products, arithmetic and copies ran while one was open for 3% -> 0% of each run, Pallas kernels for 0% -> 0%
where the time goes in v2:
time: 41.2 us; the launch traced here: 41.1 us
  Pallas kernels  38.9 us (94%)
  local copies, waits for them, and re-layouts  1.51 us (4%)
  between operations  0.64 us (2%)
    pallas_call x1, Pallas kernels, shards(): pl.pallas_call(kernel, out_shape=(result, result), in_specs=[anywhere] *...  38.9 us
    transpose x1, local copies, waits for them, and re-layouts, shards(): lower = lower.reshape(OWN, KOFF, 2, KEEP, LANE).transpose(order)  1.51 us

profile of v2, /device:TPU:6, one launch (start us, length us, event | category | flops | bytes accessed | tf_op | source)
XLA Modules:
  0.0 41.1 jit_solution(13651952610426794208)
XLA Ops:
  0.6 38.9 %spectral_pairs.1 = (f32[32,2,16,128]{3,2,1,0:T(8,128)S(1)}, f32[32,2,16,128]{3,2,1,0:T(8,128)S(1)}) custom-call(s32[4]{0:T(128)} %reach_ref.1, s32[4,8]{1,0:T(4,128)} %valid_ref.1, s32[4,128]{1,0:T(4,128)} %bitcast.11, bf16[1024,512]{1,0:T(8,128)(2,1)} %bitcast.10), custom_call_target="tpu_custom_call" | custom-call | flops 2147483648 | bytes 2097152 | tf_op jit(solution)/shard_map/spectral_pairs/pallas_call | solution.py:452
  39.6 1.5 %copy_bitcast_fusion = (f32[16,4,8,2,128]{4,3,2,1,0:T(2,128)}, f32[16,4,8,2,128]{4,3,2,1,0:T(2,128)}) fusion(f32[4,8,2,16,128]{4,3,2,1,0:T(8,128)S(1)} %bitcast.9, f32[4,8,2,16,128]{4,3,2,1,0:T(8,128)S(1)} %bitcast.8), kind=kLoop, calls=%fused_computation | loop fusion | bytes 2097152 | tf_op jit(solution)/shard_map/transpose | solution.py:466

commit v3 on v2

--- a/solution.py
+++ b/solution.py
@@ -41,7 +41,7 @@
     (("a", "xb"), ((4, 7, 6, 1),)),
     (("x", "ab"), ((5, 6, 6, 2),)),
     (("a", "xb"), ((6, 5, 6, 3),)),
-    (("b", "xa"), ((7, 4, 6, 4),)),
+    (("xab",), ((7, 4, 6, 4),)),
 )
 EVEN_STEPS = (
     "c0", "c1", "a4", "w", "c2", "a5", "c3", "a6", "c4", "a7", "c5", "p2", "c6", "m1.1", "m0.1", "m4.1",
@@ -50,7 +50,7 @@
 )
 ODD_STEPS = (
     "c0", "c1", "p2", "p1", "p0", "a4", "w", "c2", "m1.1", "a5", "c3", "m0.1", "m1.2", "a6", "c4", "m2.1",
-    "a7", "c5", "m0.2", "f1", "m3.1", "m4.1", "v", "f2", "m5.1", "f0", "f3", "f4", "f5",
+    "a7", "c5", "m0.2", "f1", "m3.1", "m4.1", "v", "f2", "f0", "f3", "f4", "f5",
 )
 
 
@@ -195,10 +195,6 @@
     send_right = [remote(column(b), staged.at[OWN + b], before) for b in range(OWN)]
     send_left = [remote(column(b), staged.at[2 * OWN + b - 1], after) for b in range(1, OWN)]
 
-    pl.semaphore_wait(barrier, 2 + len(peers) - 1)
-    for copy in send_live + send_right + send_left[::-1]:
-        copy.start()
-
     @pl.when(chan == lanes - 1)
     def _():
         live[1] = jnp.zeros_like(live[1])
@@ -237,6 +233,10 @@
         block = masked(b, 0, b)
         widen(b, block)
         turn(PREV + b, block)
+
+    pl.semaphore_wait(barrier, 2 + len(peers) - 1)
+    for copy in send_live + send_right + send_left[::-1]:
+        copy.start()
 
     send_weights = remote(weights, weights_prev, after)
 

time: 41.2 us -> 40.9 us (level)
  no operation moved by 1% of the time
where the time goes in v3:
time: 40.9 us; the launch traced here: 40.8 us
  Pallas kernels  38.6 us (94%)
  local copies, waits for them, and re-layouts  1.51 us (4%)
  between operations  0.64 us (2%)
    pallas_call x1, Pallas kernels, shards(): pl.pallas_call(kernel, out_shape=(result, result), in_specs=[anywhere] *...  38.6 us
    transpose x1, local copies, waits for them, and re-layouts, shards(): lower = lower.reshape(OWN, KOFF, 2, KEEP, LANE).transpose(order)  1.51 us

profile of v3, /device:TPU:6, one launch (start us, length us, event | category | flops | bytes accessed | tf_op | source)
XLA Modules:
  0.0 40.8 jit_solution(17770649104870072450)
XLA Ops:
  0.6 38.6 %spectral_pairs.1 = (f32[32,2,16,128]{3,2,1,0:T(8,128)S(1)}, f32[32,2,16,128]{3,2,1,0:T(8,128)S(1)}) custom-call(s32[4]{0:T(128)} %reach_ref.1, s32[4,8]{1,0:T(4,128)} %valid_ref.1, s32[4,128]{1,0:T(4,128)} %bitcast.11, bf16[1024,512]{1,0:T(8,128)(2,1)} %bitcast.10), custom_call_target="tpu_custom_call" | custom-call | flops 2147483648 | bytes 2097152 | tf_op jit(solution)/shard_map/spectral_pairs/pallas_call | solution.py:452
  39.3 1.5 %copy_bitcast_fusion = (f32[16,4,8,2,128]{4,3,2,1,0:T(2,128)}, f32[16,4,8,2,128]{4,3,2,1,0:T(2,128)}) fusion(f32[4,8,2,16,128]{4,3,2,1,0:T(8,128)S(1)} %bitcast.9, f32[4,8,2,16,128]{4,3,2,1,0:T(8,128)S(1)} %bitcast.8), kind=kLoop, calls=%fused_computation | loop fusion | bytes 2097152 | tf_op jit(solution)/shard_map/transpose | solution.py:466
